TPU v7x, 256 devices: a whole 4x4x8 slice. The times are simulated.
256 devices in a mesh: head: 16 (over x_lo, y, core), ctx: 16 (over x_hi, z).
Axes of the slice: x: 4 (x_hi: 2, x_lo: 2; x = x_hi * 2 + x_lo), y: 4, z: 8, core: 2. Of those that a mesh axis runs over, the one named last changes fastest.
Arguments:
- query_states: bfloat16 [16384, 8192], P(('head', 'ctx')), may hold values from -6 to 6
- saved_key_rows: bfloat16 [16384, 1024], P(('head', 'ctx')), may hold values from -6 to 6
- saved_value_rows: bfloat16 [16384, 1024], P(('head', 'ctx')), may hold values from -6 to 6
- attn_output: bfloat16 [16384, 8192], P(('head', 'ctx')), may hold values from -3 to 3
- out_grad: bfloat16 [16384, 8192], P(('head', 'ctx')), may hold values from -6 to 6
- log_norm: float32 [16384, 64], P(('head', 'ctx')), may hold values from 4 to 6
- block_pos: int32 [256], replicated, may hold values from 0 to 255, as said below
Outputs:
- query_grad: bfloat16 [16384, 8192], P(('head', 'ctx'))
- key_gradient: bfloat16 [16384, 1024], P(('head', 'ctx'))
- value_gradient: bfloat16 [16384, 1024], P(('head', 'ctx'))
Inputs may be any that keep to these rules, and one draw needn't show every extreme that they name: block_pos is a permutation. For each c below 16 there is an r, different for different c, such that block c + j * 16 has position r * 8 + j for j below 8, and position (31 - r) * 8 + j - 8 for the other j.
All inputs are finite; a program needn't handle non-finite values.
Results may differ from a plain program's by a relative error of at most 0.0059.
Values may be sent and summed in bfloat16 or wider, within the bound.
A program may use at most 128 MiB of HBM per device.

v0:
```python
import jax
import jax.numpy as jnp
from jax import lax
from jax.experimental import pallas as pl
from jax.experimental.pallas import tpu as pltpu
from jax.sharding import PartitionSpec as P

HQ = 64
KEY_VALUE_HEADS = 8
HEAD_SIZE = 128
BLOCK = 64
N = 16
HEADS = HQ // N
ROWS = N * BLOCK
HALF = ROWS // 2
QUARTER = ROWS // 4
FACTOR = HEAD_SIZE**-0.5
LOG2E = 1.4426950408889634
MESH = pl.DeviceIdType.MESH
F32 = jnp.float32
BF16 = jnp.bfloat16


def dot(a, b):
    return jnp.dot(a, b, preferred_element_type=F32)


def dot_t(a, b):
    return lax.dot_general(a, b, (((1,), (1,)), ((), ())), preferred_element_type=F32)


def transposed(x):
    return x.astype(F32).T.astype(BF16)


def tile(k, kt, v, q, do, norm, delta, diagonal):
    s = dot_t(k, q)
    p = jnp.exp2(s * (FACTOR * LOG2E) - norm)
    if diagonal:
        key = lax.broadcasted_iota(jnp.int32, s.shape, 0)
        query = lax.broadcasted_iota(jnp.int32, s.shape, 1)
        p = jnp.where(query >= key, p, 0.0)
    ds = (p * (dot_t(v, do) - delta)).astype(BF16)
    return dot(kt, ds), dot(ds, q), dot(p.astype(BF16), do)


def kernel(
    q, do, at, k, v, ln, bp,
    qg, kvg,
    dov, atv, kvs, st_s, st_r, srow, qd, own, prev, own_t, prev_t, sel, sel_t,
    acc_own, acc_prev, acc_sel, dq_t, dq_s, x_s, x_r, ctx_s, ctx_r, y_s, y_r, fin,
    s_load, s_kv, r_kv, s_fw, r_fw, s_ctx, r_ctx, s_fwp, r_fwp, s_st, r_st, s_qd, r_qd,
    s_x, r_x, s_back, r_back, s_y, r_y, s_dq, r_dq, s_fin, r_fin,
):
    h = lax.axis_index("head")
    c = lax.axis_index("ctx")
    g = lax.div(h, 2)
    m = lax.rem(h, 2)
    mate = h + 1 - 2 * m
    after = lax.rem(c + 1, N)
    before = lax.rem(c + N - 1, N)

    def remote(src, dst, ssem, rsem, **where):
        return pltpu.make_async_remote_copy(
            src_ref=src, dst_ref=dst, send_sem=ssem, recv_sem=rsem, device_id=where, device_id_type=MESH
        )

    def wait(ref, sem):
        pltpu.make_async_copy(ref, ref, sem).wait()

    def cols(j):
        return pl.ds(pl.multiple_of(j * HEAD_SIZE, HEAD_SIZE), HEAD_SIZE)

    def rows(j):
        return pl.ds(pl.multiple_of(j * BLOCK, BLOCK), BLOCK)

    loads = [
        pltpu.make_async_copy(k, kvs.at[0], s_load.at[0]),
        pltpu.make_async_copy(v, kvs.at[1], s_load.at[1]),
        pltpu.make_async_copy(do, dov, s_load.at[2]),
        pltpu.make_async_copy(at, atv, s_load.at[3]),
    ]
    for copy in loads:
        copy.start()

    barrier = pltpu.get_barrier_semaphore()

    @pl.loop(1, N)
    def _(s):
        pl.semaphore_signal(barrier, inc=1, device_id={"head": lax.rem(h + s, N)}, device_id_type=MESH)

    pl.semaphore_signal(barrier, inc=1, device_id={"ctx": after}, device_id_type=MESH)
    pl.semaphore_signal(barrier, inc=1, device_id={"ctx": before}, device_id_type=MESH)
    loads[0].wait()
    loads[1].wait()
    pl.semaphore_wait(barrier, N + 1)

    @pl.loop(1, N)
    def _(s):
        d = lax.rem(h + s, N)
        e = lax.rem(d, 2)
        remote(kvs.at[e, :, cols(lax.div(d, 2))], own.at[e, rows(h)], s_kv, r_kv, head=d).start()

    pltpu.make_async_copy(kvs.at[m, :, cols(g)], own.at[m, rows(h)], r_kv).start()

    def send_head(i):
        @pl.loop(1, N)
        def _(s):
            d = lax.rem(h + s, N)
            for which, ref in ((0, q), (1, do)):
                remote(
                    ref.at[:, cols(d * HEADS + i)], qd.at[i, which, rows(h)], s_qd.at[i], r_qd.at[i], head=d
                ).start()

        for which, ref in ((0, q), (1, do)):
            pltpu.make_async_copy(ref.at[:, cols(h * HEADS + i)], qd.at[i, which, rows(h)], r_qd.at[i]).start()

    send_head(0)

    loads[2].wait()
    loads[3].wait()
    lane = lax.broadcasted_iota(jnp.int32, (BLOCK, 2 * BLOCK), 1)

    def inner(j, total):
        part = jnp.sum(dov[:, cols(j)].astype(F32) * atv[:, cols(j)].astype(F32), axis=1, keepdims=True)
        return jnp.where(lane == j, part, total)

    deltas = lax.fori_loop(0, HQ, inner, jnp.zeros((BLOCK, 2 * BLOCK), F32), unroll=8)
    stats = jnp.where(lane < BLOCK, deltas, jnp.concatenate([ln[...], ln[...]], axis=1) * LOG2E).T
    stats = jnp.concatenate([stats, stats], axis=1)
    for d in range(N):
        st_s[d, 0:HEADS] = stats[HQ + d * HEADS : HQ + (d + 1) * HEADS]
        st_s[d, HEADS:] = stats[d * HEADS : (d + 1) * HEADS]

    @pl.loop(1, N)
    def _(s):
        d = lax.rem(h + s, N)
        remote(st_s.at[d], st_r.at[h], s_st, r_st, head=d).start()

    pltpu.make_async_copy(st_s.at[h], st_r.at[h], r_st).start()

    @pl.loop(1, HEADS)
    def _(i):
        send_head(i)

    wait(own.at[0], r_kv)
    forward = remote(own.at[m], own.at[m], s_fw, r_fw, head=mate)
    forward.start()
    onward = remote(own.at[m], prev.at[m], s_ctx, r_ctx, ctx=after)
    onward.start()
    forward.wait_recv()
    own_t[...] = transposed(own[0])

    wait(st_r, r_st)
    wide = lax.broadcasted_iota(jnp.int32, (2 * HEADS, 2 * BLOCK), 1)
    for pair in range(N // 2):
        srow[:, pair * 128 : (pair + 1) * 128] = jnp.where(wide < BLOCK, st_r[2 * pair], st_r[2 * pair + 1])

    onward.wait_recv()
    forward_prev = remote(prev.at[m], prev.at[m], s_fwp, r_fwp, head=mate)
    forward_prev.start()
    acc_own[...] = jnp.zeros_like(acc_own)
    acc_prev[...] = jnp.zeros_like(acc_prev)
    acc_sel[...] = jnp.zeros_like(acc_sel)
    forward_prev.wait_recv()

    early = bp[c] > bp[before]
    for which in range(2):
        sel[which] = jnp.where(early, prev[which, :HALF], prev[which, HALF:])
    prev_t[...] = transposed(prev[0, :HALF])
    sel_t[...] = transposed(sel[0])

    def add(ref, lo, size, dk, dv):
        ref[0, lo : lo + size] += dk
        ref[1, lo : lo + size] += dv

    def row(i, lo, size):
        return srow[pl.ds(i, 1), lo : lo + size], srow[pl.ds(HEADS + i, 1), lo : lo + size]

    def combined(which):
        chosen = acc_sel[which]
        zero = jnp.zeros_like(chosen)
        low = acc_prev[which] + jnp.where(early, chosen, zero)
        return low, jnp.where(early, zero, chosen)

    @pl.loop(0, HEADS)
    def _(i):
        wait(qd.at[i], r_qd.at[i])
        q_sel = jnp.where(early, qd[i, 0, :HALF], qd[i, 0, HALF:])
        do_sel = jnp.where(early, qd[i, 1, :HALF], qd[i, 1, HALF:])
        n0, d0 = row(i, 0, HALF)
        n1, d1 = row(i, HALF, HALF)
        dq, dk, dv = tile(
            sel[0], sel_t[...], sel[1], q_sel, do_sel, jnp.where(early, n0, n1), jnp.where(early, d0, d1), False
        )
        add(acc_sel, 0, HALF, dk, dv)
        zero = jnp.zeros_like(dq)
        dq_t[:, :HALF] = jnp.where(early, dq, zero)
        dq_t[:, HALF:] = jnp.where(early, zero, dq)
        dq, dk, dv = tile(
            prev[0, :HALF], prev_t[...], prev[1, :HALF], qd[i, 0, HALF:], qd[i, 1, HALF:], n1, d1, False
        )
        add(acc_prev, 0, HALF, dk, dv)
        dq_t[:, HALF:] += dq

        @pl.when(i == HEADS - 1)
        def _():
            low, high = combined(1 - m)
            x_s[:HALF] = low.astype(BF16)
            x_s[HALF:] = high.astype(BF16)
            remote(x_s, x_r, s_x, r_x, head=mate).start()

        dq, dk, dv = tile(
            own[0, :HALF], own_t[:, :HALF], own[1, :HALF], qd[i, 0, HALF:], qd[i, 1, HALF:], n1, d1, False
        )
        add(acc_own, 0, HALF, dk, dv)
        dq_t[:, HALF:] += dq

        @pl.when(i == HEADS - 1)
        def _():
            wait(x_r, r_x)
            low, high = combined(m)
            scale = jnp.where(m == 0, FACTOR, 1.0)
            ctx_s[:HALF] = ((low + x_r[:HALF].astype(F32)) * scale).astype(BF16)
            ctx_s[HALF:] = ((high + x_r[HALF:].astype(F32)) * scale).astype(BF16)
            remote(ctx_s, ctx_r, s_back, r_back, ctx=before).start()

        for kb, qb, size in ((0, 0, 1), (0, 1, 1), (1, 1, 1), (2, 2, 1), (2, 3, 1), (3, 3, 1)):
            ks = slice(kb * QUARTER, (kb + size) * QUARTER)
            qs = slice(qb * QUARTER, (qb + size) * QUARTER)
            nn, dd = row(i, qb * QUARTER, QUARTER)
            dq, dk, dv = tile(own[0, ks], own_t[:, ks], own[1, ks], qd[i, 0, qs], qd[i, 1, qs], nn, dd, kb == qb)
            add(acc_own, kb * QUARTER, QUARTER, dk, dv)
            dq_t[:, qs] += dq

        dq_s[i] = (dq_t[...] * FACTOR).T.astype(BF16)

        @pl.loop(1, N)
        def _(s):
            d = lax.rem(h + s, N)
            remote(dq_s.at[i, rows(d)], qg.at[:, cols(h * HEADS + i)], s_dq, r_dq, head=d).start()

        pltpu.make_async_copy(dq_s.at[i, rows(h)], qg.at[:, cols(h * HEADS + i)], r_dq).start()

    y_s[...] = acc_own[1 - m].astype(BF16)
    remote(y_s, y_r, s_y, r_y, head=mate).start()
    wait(y_r, r_y)
    wait(ctx_r, r_back)
    scale = jnp.where(m == 0, FACTOR, 1.0)
    fin[...] = ((acc_own[m] + y_r[...].astype(F32)) * scale + ctx_r[...].astype(F32)).astype(BF16)

    @pl.loop(1, N)
    def _(s):
        d = lax.rem(h + s, N)
        remote(fin.at[rows(d)], kvg.at[m, :, cols(g)], s_fin, r_fin, head=d).start()

    pltpu.make_async_copy(fin.at[rows(h)], kvg.at[m, :, cols(g)], r_fin).start()

    most = (N - 1) * BLOCK
    wait(own.at[0, :most], s_kv)
    forward.wait_send()
    onward.wait_send()
    forward_prev.wait_send()
    wait(st_r.at[: N - 1], s_st)
    for i in range(HEADS):
        wait(qd.at[i, :, :most], s_qd.at[i])
    wait(x_s, s_x)
    wait(ctx_s, s_back)
    wait(y_s, s_y)
    wait(dq_s.at[:, :most], s_dq)
    wait(fin.at[:most], s_fin)
    wait(qg, r_dq)
    wait(kvg, r_fin)


def shards(query_states, saved_key_rows, saved_value_rows, attn_output, out_grad, log_norm, block_pos):
    hbm = pl.BlockSpec(memory_space=pl.ANY)
    dma = pltpu.SemaphoreType.DMA
    half = lambda *lead: pltpu.VMEM((*lead, HALF, HEAD_SIZE), BF16)
    full = lambda *lead: pltpu.VMEM((*lead, ROWS, HEAD_SIZE), BF16)
    qg, kvg = pl.pallas_call(
        kernel,
        out_shape=(
            jax.ShapeDtypeStruct((BLOCK, HQ * HEAD_SIZE), BF16),
            jax.ShapeDtypeStruct((2, BLOCK, KEY_VALUE_HEADS * HEAD_SIZE), BF16),
        ),
        in_specs=[hbm] * 5 + [pl.BlockSpec(memory_space=pltpu.VMEM), pl.BlockSpec(memory_space=pltpu.SMEM)],
        out_specs=(hbm, hbm),
        scratch_shapes=[
            pltpu.VMEM((BLOCK, HQ * HEAD_SIZE), BF16),
            pltpu.VMEM((BLOCK, HQ * HEAD_SIZE), BF16),
            pltpu.VMEM((2, BLOCK, KEY_VALUE_HEADS * HEAD_SIZE), BF16),
            pltpu.VMEM((N, 2 * HEADS, 2 * BLOCK), F32),
            pltpu.VMEM((N, 2 * HEADS, 2 * BLOCK), F32),
            pltpu.VMEM((2 * HEADS, ROWS), F32),
            full(HEADS, 2),
            full(2),
            full(2),
            pltpu.VMEM((HEAD_SIZE, ROWS), BF16),
            pltpu.VMEM((HEAD_SIZE, HALF), BF16),
            half(2),
            pltpu.VMEM((HEAD_SIZE, HALF), BF16),
            pltpu.VMEM((2, ROWS, HEAD_SIZE), F32),
            pltpu.VMEM((2, HALF, HEAD_SIZE), F32),
            pltpu.VMEM((2, HALF, HEAD_SIZE), F32),
            pltpu.VMEM((HEAD_SIZE, ROWS), F32),
            full(HEADS),
            full(),
            full(),
            full(),
            full(),
            full(),
            full(),
            full(),
            dma((4,)),
            dma, dma, dma, dma, dma, dma, dma, dma, dma, dma,
            dma((HEADS,)), dma((HEADS,)),
            dma, dma, dma, dma, dma, dma, dma, dma, dma, dma,
        ],
        compiler_params=pltpu.CompilerParams(
            collective_id=1, has_side_effects=True, vmem_limit_bytes=48 << 20
        ),
        name="attention_backward",
    )(query_states, out_grad, attn_output, saved_key_rows, saved_value_rows, log_norm, block_pos)
    return qg, kvg[0], kvg[1]


def solution(mesh):
    tokens = P(("head", "ctx"), None)
    return jax.shard_map(
        shards,
        mesh=mesh,
        in_specs=(tokens,) * 6 + (P(),),
        out_specs=(tokens,) * 3,
        check_vma=False,
    )
```

profile of v0, /device:TPU:1, one launch (start us, length us, event | category | flops | bytes accessed | tf_op | source)
XLA Modules:
  0.0 68.9 jit_solution(17317580314745063571)
XLA Ops:
  0.6 0.0 copy-start
  0.6 1.2 %copy-done = bf16[64,8192]{1,0:T(8,128)(2,1)S(1)} copy-done((bf16[64,8192]{1,0:T(8,128)(2,1)S(1)}, bf16[64,8192]{1,0:T(8,128)(2,1)}, u32[]{:S(2)}) %copy-start) | copy-done | bytes 1048600
  1.9 0.0 copy-start.1
  1.9 1.2 %copy-done.1 = bf16[64,8192]{1,0:T(8,128)(2,1)S(1)} copy-done((bf16[64,8192]{1,0:T(8,128)(2,1)S(1)}, bf16[64,8192]{1,0:T(8,128)(2,1)}, u32[]{:S(2)}) %copy-start.1) | copy-done | bytes 1048600
  3.1 0.0 copy-start.2
  3.1 1.2 %copy-done.2 = bf16[64,8192]{1,0:T(8,128)(2,1)S(1)} copy-done((bf16[64,8192]{1,0:T(8,128)(2,1)S(1)}, bf16[64,8192]{1,0:T(8,128)(2,1)}, u32[]{:S(2)}) %copy-start.2) | copy-done | bytes 1048600
  4.3 0.0 copy-start.3
  4.3 0.9 %copy-done.3 = bf16[64,1024]{1,0:T(8,128)(2,1)S(1)} copy-done((bf16[64,1024]{1,0:T(8,128)(2,1)S(1)}, bf16[64,1024]{1,0:T(8,128)(2,1)}, u32[]{:S(2)}) %copy-start.3) | copy-done | bytes 131096
  5.2 0.0 copy-start.4
  5.2 0.9 %copy-done.4 = bf16[64,1024]{1,0:T(8,128)(2,1)S(1)} copy-done((bf16[64,1024]{1,0:T(8,128)(2,1)S(1)}, bf16[64,1024]{1,0:T(8,128)(2,1)}, u32[]{:S(2)}) %copy-start.4) | copy-done | bytes 131096
  6.1 0.0 copy-start.5
  6.1 0.8 %copy-done.5 = f32[64,64]{1,0:T(8,128)S(1)} copy-done((f32[64,64]{1,0:T(8,128)S(1)}, f32[64,64]{1,0:T(8,128)}, u32[]{:S(2)}) %copy-start.5) | copy-done | bytes 16408
  6.9 0.0 copy-start.6
  6.9 0.7 copy-done.6
  7.6 59.6 %attention_backward.1 = (bf16[64,8192]{1,0:T(8,128)(2,1)S(1)}, bf16[2,64,1024]{2,1,0:T(8,128)(2,1)S(1)}) custom-call(bf16[64,8192]{1,0:T(8,128)(2,1)S(1)} %copy-done, bf16[64,8192]{1,0:T(8,128)(2,1)S(1)} %copy-done.1, bf16[64,8192]{1,0:T(8,128)(2,1)S(1)} %copy-done.2, bf16[64,1024]{1,0:T(8,128)(2,1)S(1)} %copy-done.3, bf16[64,1024]{1,0:T(8,128)(2,1)S(1)} %copy-done.4, ...), custom_call_target="tpu_custom_call" | custom-call | tf_op jit(solution)/shard_map/attention_backward/pallas_call | solution.py:281
  67.2 0.7 %slice_bitcast_fusion = (bf16[64,1024]{1,0:T(8,128)(2,1)}, bf16[64,1024]{1,0:T(8,128)(2,1)}) fusion(bf16[2,64,1024]{2,1,0:T(8,128)(2,1)S(1)} %get-tuple-element.6), kind=kLoop, calls=%fused_computation | loop fusion | bytes 524288 | tf_op jit(solution)/shard_map/squeeze | solution.py:325
  67.9 1.0 %copy.11 = bf16[64,8192]{1,0:T(8,128)(2,1)} copy(bf16[64,8192]{1,0:T(8,128)(2,1)S(1)} %get-tuple-element.12) | data formatting | bytes 2097152
Async XLA Ops:
  0.6 1.2 %copy-start = (bf16[64,8192]{1,0:T(8,128)(2,1)S(1)}, bf16[64,8192]{1,0:T(8,128)(2,1)}, u32[]{:S(2)}) copy-start(bf16[64,8192]{1,0:T(8,128)(2,1)} %q.1) | copy-start | bytes 3145732
  1.9 1.2 %copy-start.1 = (bf16[64,8192]{1,0:T(8,128)(2,1)S(1)}, bf16[64,8192]{1,0:T(8,128)(2,1)}, u32[]{:S(2)}) copy-start(bf16[64,8192]{1,0:T(8,128)(2,1)} %do.1) | copy-start | bytes 3145732
  3.1 1.2 %copy-start.2 = (bf16[64,8192]{1,0:T(8,128)(2,1)S(1)}, bf16[64,8192]{1,0:T(8,128)(2,1)}, u32[]{:S(2)}) copy-start(bf16[64,8192]{1,0:T(8,128)(2,1)} %at.1) | copy-start | bytes 3145732
  4.3 0.9 %copy-start.3 = (bf16[64,1024]{1,0:T(8,128)(2,1)S(1)}, bf16[64,1024]{1,0:T(8,128)(2,1)}, u32[]{:S(2)}) copy-start(bf16[64,1024]{1,0:T(8,128)(2,1)} %k.1) | copy-start | bytes 393220
  5.2 0.9 %copy-start.4 = (bf16[64,1024]{1,0:T(8,128)(2,1)S(1)}, bf16[64,1024]{1,0:T(8,128)(2,1)}, u32[]{:S(2)}) copy-start(bf16[64,1024]{1,0:T(8,128)(2,1)} %v.1) | copy-start | bytes 393220
  6.1 0.8 %copy-start.5 = (f32[64,64]{1,0:T(8,128)S(1)}, f32[64,64]{1,0:T(8,128)}, u32[]{:S(2)}) copy-start(f32[64,64]{1,0:T(8,128)} %ln.1) | copy-start | bytes 49156
  6.9 0.7 copy-start.6
where the time goes:
time: 69.2 us; the launch traced here: 68.9 us
  Pallas kernels  59.6 us (86%)
  local copies, waits for them, and re-layouts  8.6 us (12%)
    pallas_call x1, Pallas kernels, shards(): pl.pallas_call(kernel, out_shape=(jax.ShapeDtypeStruct((BLOCK, HQ * HEAD_...  59.6 us
    unnamed x15, local copies, waits for them, and re-layouts  7.88 us

commit v1 on v0

--- a/solution.py
+++ b/solution.py
@@ -45,20 +45,24 @@
 
 
 def kernel(
-    q, do, at, k, v, ln, bp,
+    q, do, at, k, v, log_norm, block_pos,
     qg, kvg,
-    dov, atv, kvs, st_s, st_r, srow, qd, own, prev, own_t, prev_t, sel, sel_t,
+    ln, bp, dov, atv, kvs, st_s, st_r, srow, qd, own, prev, own_t, prev_t, sel, sel_t,
     acc_own, acc_prev, acc_sel, dq_t, dq_s, x_s, x_r, ctx_s, ctx_r, y_s, y_r, fin,
     s_load, s_kv, r_kv, s_fw, r_fw, s_ctx, r_ctx, s_fwp, r_fwp, s_st, r_st, s_qd, r_qd,
     s_x, r_x, s_back, r_back, s_y, r_y, s_dq, r_dq, s_fin, r_fin,
 ):
     h = lax.axis_index("head")
     c = lax.axis_index("ctx")
-    g = lax.div(h, 2)
+    shift = lax.div(c, N // 2) * (N // 2)
+    mine = lax.rem(h + shift, N)
+    g = lax.div(mine, 2)
     m = lax.rem(h, 2)
     mate = h + 1 - 2 * m
     after = lax.rem(c + 1, N)
     before = lax.rem(c + N - 1, N)
+    h_after = lax.rem(h + lax.div(lax.rem(c, N // 2) + 1, N // 2) * (N // 2), N)
+    h_before = lax.rem(h + lax.div(lax.rem(before, N // 2) + 1, N // 2) * (N // 2), N)
 
     def remote(src, dst, ssem, rsem, **where):
         return pltpu.make_async_remote_copy(
@@ -79,6 +83,8 @@
         pltpu.make_async_copy(v, kvs.at[1], s_load.at[1]),
         pltpu.make_async_copy(do, dov, s_load.at[2]),
         pltpu.make_async_copy(at, atv, s_load.at[3]),
+        pltpu.make_async_copy(log_norm, ln, s_load.at[4]),
+        pltpu.make_async_copy(block_pos, bp, s_load.at[5]),
     ]
     for copy in loads:
         copy.start()
@@ -89,8 +95,8 @@
     def _(s):
         pl.semaphore_signal(barrier, inc=1, device_id={"head": lax.rem(h + s, N)}, device_id_type=MESH)
 
-    pl.semaphore_signal(barrier, inc=1, device_id={"ctx": after}, device_id_type=MESH)
-    pl.semaphore_signal(barrier, inc=1, device_id={"ctx": before}, device_id_type=MESH)
+    pl.semaphore_signal(barrier, inc=1, device_id={"head": h_after, "ctx": after}, device_id_type=MESH)
+    pl.semaphore_signal(barrier, inc=1, device_id={"head": h_before, "ctx": before}, device_id_type=MESH)
     loads[0].wait()
     loads[1].wait()
     pl.semaphore_wait(barrier, N + 1)
@@ -99,7 +105,7 @@
     def _(s):
         d = lax.rem(h + s, N)
         e = lax.rem(d, 2)
-        remote(kvs.at[e, :, cols(lax.div(d, 2))], own.at[e, rows(h)], s_kv, r_kv, head=d).start()
+        remote(kvs.at[e, :, cols(lax.div(lax.rem(d + shift, N), 2))], own.at[e, rows(h)], s_kv, r_kv, head=d).start()
 
     pltpu.make_async_copy(kvs.at[m, :, cols(g)], own.at[m, rows(h)], r_kv).start()
 
@@ -109,16 +115,16 @@
             d = lax.rem(h + s, N)
             for which, ref in ((0, q), (1, do)):
                 remote(
-                    ref.at[:, cols(d * HEADS + i)], qd.at[i, which, rows(h)], s_qd.at[i], r_qd.at[i], head=d
+                    ref.at[:, cols(lax.rem(d + shift, N) * HEADS + i)], qd.at[i, which, rows(h)], s_qd.at[i], r_qd.at[i], head=d
                 ).start()
 
         for which, ref in ((0, q), (1, do)):
-            pltpu.make_async_copy(ref.at[:, cols(h * HEADS + i)], qd.at[i, which, rows(h)], r_qd.at[i]).start()
+            pltpu.make_async_copy(ref.at[:, cols(mine * HEADS + i)], qd.at[i, which, rows(h)], r_qd.at[i]).start()
 
     send_head(0)
 
-    loads[2].wait()
-    loads[3].wait()
+    for copy in loads[2:]:
+        copy.wait()
     lane = lax.broadcasted_iota(jnp.int32, (BLOCK, 2 * BLOCK), 1)
 
     def inner(j, total):
@@ -135,9 +141,9 @@
     @pl.loop(1, N)
     def _(s):
         d = lax.rem(h + s, N)
-        remote(st_s.at[d], st_r.at[h], s_st, r_st, head=d).start()
-
-    pltpu.make_async_copy(st_s.at[h], st_r.at[h], r_st).start()
+        remote(st_s.at[lax.rem(d + shift, N)], st_r.at[h], s_st, r_st, head=d).start()
+
+    pltpu.make_async_copy(st_s.at[mine], st_r.at[h], r_st).start()
 
     @pl.loop(1, HEADS)
     def _(i):
@@ -146,7 +152,7 @@
     wait(own.at[0], r_kv)
     forward = remote(own.at[m], own.at[m], s_fw, r_fw, head=mate)
     forward.start()
-    onward = remote(own.at[m], prev.at[m], s_ctx, r_ctx, ctx=after)
+    onward = remote(own.at[m], prev.at[m], s_ctx, r_ctx, head=h_after, ctx=after)
     onward.start()
     forward.wait_recv()
     own_t[...] = transposed(own[0])
@@ -223,7 +229,7 @@
             scale = jnp.where(m == 0, FACTOR, 1.0)
             ctx_s[:HALF] = ((low + x_r[:HALF].astype(F32)) * scale).astype(BF16)
             ctx_s[HALF:] = ((high + x_r[HALF:].astype(F32)) * scale).astype(BF16)
-            remote(ctx_s, ctx_r, s_back, r_back, ctx=before).start()
+            remote(ctx_s, ctx_r, s_back, r_back, head=h_before, ctx=before).start()
 
         for kb, qb, size in ((0, 0, 1), (0, 1, 1), (1, 1, 1), (2, 2, 1), (2, 3, 1), (3, 3, 1)):
             ks = slice(kb * QUARTER, (kb + size) * QUARTER)
@@ -238,9 +244,9 @@
         @pl.loop(1, N)
         def _(s):
             d = lax.rem(h + s, N)
-            remote(dq_s.at[i, rows(d)], qg.at[:, cols(h * HEADS + i)], s_dq, r_dq, head=d).start()
-
-        pltpu.make_async_copy(dq_s.at[i, rows(h)], qg.at[:, cols(h * HEADS + i)], r_dq).start()
+            remote(dq_s.at[i, rows(d)], qg.at[:, cols(mine * HEADS + i)], s_dq, r_dq, head=d).start()
+
+        pltpu.make_async_copy(dq_s.at[i, rows(h)], qg.at[:, cols(mine * HEADS + i)], r_dq).start()
 
     y_s[...] = acc_own[1 - m].astype(BF16)
     remote(y_s, y_r, s_y, r_y, head=mate).start()
@@ -274,19 +280,24 @@
 
 
 def shards(query_states, saved_key_rows, saved_value_rows, attn_output, out_grad, log_norm, block_pos):
-    hbm = pl.BlockSpec(memory_space=pl.ANY)
+    hbm = pl.BlockSpec(memory_space=pltpu.HBM)
+    vmem = pl.BlockSpec(memory_space=pltpu.VMEM)
+    inputs = (query_states, out_grad, attn_output, saved_key_rows, saved_value_rows, log_norm, block_pos)
+    inputs = tuple(pltpu.with_memory_space_constraint(x, pltpu.HBM) for x in inputs)
     dma = pltpu.SemaphoreType.DMA
     half = lambda *lead: pltpu.VMEM((*lead, HALF, HEAD_SIZE), BF16)
     full = lambda *lead: pltpu.VMEM((*lead, ROWS, HEAD_SIZE), BF16)
     qg, kvg = pl.pallas_call(
         kernel,
         out_shape=(
-            jax.ShapeDtypeStruct((BLOCK, HQ * HEAD_SIZE), BF16),
-            jax.ShapeDtypeStruct((2, BLOCK, KEY_VALUE_HEADS * HEAD_SIZE), BF16),
+            pltpu.VMEM((BLOCK, HQ * HEAD_SIZE), BF16),
+            pltpu.VMEM((2, BLOCK, KEY_VALUE_HEADS * HEAD_SIZE), BF16),
         ),
-        in_specs=[hbm] * 5 + [pl.BlockSpec(memory_space=pltpu.VMEM), pl.BlockSpec(memory_space=pltpu.SMEM)],
-        out_specs=(hbm, hbm),
+        in_specs=[hbm] * 7,
+        out_specs=(vmem, vmem),
         scratch_shapes=[
+            pltpu.VMEM((BLOCK, HQ), F32),
+            pltpu.SMEM((N * N,), jnp.int32),
             pltpu.VMEM((BLOCK, HQ * HEAD_SIZE), BF16),
             pltpu.VMEM((BLOCK, HQ * HEAD_SIZE), BF16),
             pltpu.VMEM((2, BLOCK, KEY_VALUE_HEADS * HEAD_SIZE), BF16),
@@ -312,7 +323,7 @@
             full(),
             full(),
             full(),
-            dma((4,)),
+            dma((6,)),
             dma, dma, dma, dma, dma, dma, dma, dma, dma, dma,
             dma((HEADS,)), dma((HEADS,)),
             dma, dma, dma, dma, dma, dma, dma, dma, dma, dma,
@@ -321,7 +332,7 @@
             collective_id=1, has_side_effects=True, vmem_limit_bytes=48 << 20
         ),
         name="attention_backward",
-    )(query_states, out_grad, attn_output, saved_key_rows, saved_value_rows, log_norm, block_pos)
+    )(*inputs)
     return qg, kvg[0], kvg[1]
 
 

time: 69.2 us -> 57.4 us (0.83)
  local copies, waits for them, and re-layouts: 8.6 us -> 1.69 us
  Pallas kernels: 59.6 us -> 55 us
    unnamed x15 -> x1, local copies, waits for them, and re-layouts: 7.88 us -> 0.97 us
    pallas_call x1, Pallas kernels: 59.6 us -> 55 us  [shards(): pl.pallas_call(kernel, out_shape=(pltpu.VMEM((BLOCK, HQ * HEAD_SIZE), BF1...]
where the time goes in v1:
time: 57.4 us; the launch traced here: 57.3 us
  Pallas kernels  55 us (96%)
  local copies, waits for them, and re-layouts  1.69 us (3%)
  between operations  0.64 us (1%)
    pallas_call x1, Pallas kernels, shards(): pl.pallas_call(kernel, out_shape=(pltpu.VMEM((BLOCK, HQ * HEAD_SIZE), BF1...  55 us

profile of v1, /device:TPU:1, one launch (start us, length us, event | category | flops | bytes accessed | tf_op | source)
XLA Modules:
  0.0 57.3 jit_solution(15937339852173967890)
XLA Ops:
  0.6 55.0 %attention_backward.1 = (bf16[64,8192]{1,0:T(8,128)(2,1)S(1)}, bf16[2,64,1024]{2,1,0:T(8,128)(2,1)S(1)}) custom-call(bf16[64,8192]{1,0:T(8,128)(2,1)} %q.1, bf16[64,8192]{1,0:T(8,128)(2,1)} %do.1, bf16[64,8192]{1,0:T(8,128)(2,1)} %at.1, bf16[64,1024]{1,0:T(8,128)(2,1)} %k.1, bf16[64,1024]{1,0:T(8,128)(2,1)} %v.1, f32[64,64]{1,0:T(8,128)} %log_norm.1, ...), custom_call_target="tpu_custom_call" | custom-call | tf_op jit(solution)/shard_map/attention_backward/pallas_call | solution.py:290
  55.6 1.0 %copy.11 = bf16[64,8192]{1,0:T(8,128)(2,1)} copy(bf16[64,8192]{1,0:T(8,128)(2,1)S(1)} %get-tuple-element.9) | data formatting | bytes 2097152
  56.6 0.7 %slice_bitcast_fusion = (bf16[64,1024]{1,0:T(8,128)(2,1)}, bf16[64,1024]{1,0:T(8,128)(2,1)}) fusion(bf16[2,64,1024]{2,1,0:T(8,128)(2,1)S(1)} %get-tuple-element.6), kind=kLoop, calls=%fused_computation | loop fusion | bytes 524288 | tf_op jit(solution)/shard_map/squeeze | solution.py:336

commit v2 on v1

v2 whole, which is shorter than its diff:
```python
import jax
import jax.numpy as jnp
from jax import lax
from jax.experimental import pallas as pl
from jax.experimental.pallas import tpu as pltpu
from jax.sharding import PartitionSpec as P

HQ = 64
KEY_VALUE_HEADS = 8
HEAD_SIZE = 128
BLOCK = 64
N = 16
HEADS = HQ // N
ROWS = N * BLOCK
HALF = ROWS // 2
QUARTER = ROWS // 4
PIECES = 4
FACTOR = HEAD_SIZE**-0.5
LOG2E = 1.4426950408889634
MESH = pl.DeviceIdType.MESH
F32 = jnp.float32
BF16 = jnp.bfloat16


def dot(a, b):
    return jnp.dot(a, b, preferred_element_type=F32)


def dot_t(a, b):
    return lax.dot_general(a, b, (((1,), (1,)), ((), ())), preferred_element_type=F32)


def transposed(x):
    return x.astype(F32).T.astype(BF16)


def scores(k, v, q, do):
    return dot_t(k, q), dot_t(v, do)


def terms(front, kt, q, do, norm, delta, diagonal):
    s, dp = front
    p = jnp.exp2(s * (FACTOR * LOG2E) - norm)
    if diagonal:
        key = lax.broadcasted_iota(jnp.int32, s.shape, 0)
        query = lax.broadcasted_iota(jnp.int32, s.shape, 1)
        p = jnp.where(query >= key, p, 0.0)
    ds = (p * (dp - delta)).astype(BF16)
    p = p.astype(BF16)
    dv = dot(p, do)
    dk = dot(ds, q)
    return dot(kt, ds), dk, dv


def in_turn(tiles):
    ahead = scores(*tiles[0][0])
    for n, (_, rest, keep) in enumerate(tiles):
        front = ahead
        if n + 1 < len(tiles):
            ahead = scores(*tiles[n + 1][0])
        keep(*terms(front, *rest))


def kernel(
    q, do, at, k, v, log_norm, block_pos,
    qg, kvg,
    ln, bp, dov, atv, kvs, st_s, st_r, srow, qd, own, prev, own_t, prev_t, sel, sel_t,
    acc_own, acc_prev, acc_sel, dq_t, dq_s, x_s, x_r, ctx_s, ctx_r, y_s, y_r, fin,
    s_load, s_kv, r_kv, s_fw, r_fw, s_ctx, r_ctx, s_fwp, r_fwp, s_st, r_st, s_qd, r_qd,
    s_x, r_x, s_back, r_back, s_y, r_y, s_dq, r_dq, s_fin, r_fin,
):
    h = lax.axis_index("head")
    c = lax.axis_index("ctx")
    shift = lax.div(c, N // 2) * (N // 2)
    mine = lax.rem(h + shift, N)
    g = lax.div(mine, 2)
    m = lax.rem(h, 2)
    mate = h + 1 - 2 * m
    after = lax.rem(c + 1, N)
    before = lax.rem(c + N - 1, N)
    h_after = lax.rem(h + lax.div(lax.rem(c, N // 2) + 1, N // 2) * (N // 2), N)
    h_before = lax.rem(h + lax.div(lax.rem(before, N // 2) + 1, N // 2) * (N // 2), N)

    def remote(src, dst, ssem, rsem, **where):
        return pltpu.make_async_remote_copy(
            src_ref=src, dst_ref=dst, send_sem=ssem, recv_sem=rsem, device_id=where, device_id_type=MESH
        )

    def wait(ref, sem):
        pltpu.make_async_copy(ref, ref, sem).wait()

    def cols(j):
        return pl.ds(pl.multiple_of(j * HEAD_SIZE, HEAD_SIZE), HEAD_SIZE)

    def rows(j):
        return pl.ds(pl.multiple_of(j * BLOCK, BLOCK), BLOCK)

    loads = [
        pltpu.make_async_copy(k, kvs.at[0], s_load.at[0]),
        pltpu.make_async_copy(v, kvs.at[1], s_load.at[1]),
        pltpu.make_async_copy(do, dov, s_load.at[2]),
        pltpu.make_async_copy(at, atv, s_load.at[3]),
        pltpu.make_async_copy(log_norm, ln, s_load.at[4]),
        pltpu.make_async_copy(block_pos, bp, s_load.at[5]),
    ]
    for copy in loads:
        copy.start()

    barrier = pltpu.get_barrier_semaphore()

    @pl.loop(1, N)
    def _(s):
        pl.semaphore_signal(barrier, inc=1, device_id={"head": lax.rem(h + s, N)}, device_id_type=MESH)

    pl.semaphore_signal(barrier, inc=1, device_id={"head": h_before, "ctx": before}, device_id_type=MESH)
    loads[0].wait()
    loads[1].wait()
    pl.semaphore_wait(barrier, N)

    @pl.loop(1, N)
    def _(s):
        d = lax.rem(h + s, N)
        e = lax.rem(d, 2)
        remote(kvs.at[e, :, cols(lax.div(lax.rem(d + shift, N), 2))], own.at[e, rows(h)], s_kv, r_kv, head=d).start()

    pltpu.make_async_copy(kvs.at[m, :, cols(g)], own.at[m, rows(h)], r_kv).start()

    def send_head(i):
        @pl.loop(1, N)
        def _(s):
            d = lax.rem(h + s, N)
            for which, ref in ((0, q), (1, do)):
                remote(
                    ref.at[:, cols(lax.rem(d + shift, N) * HEADS + i)], qd.at[i, which, rows(h)], s_qd.at[i], r_qd.at[i], head=d
                ).start()

        for which, ref in ((0, q), (1, do)):
            pltpu.make_async_copy(ref.at[:, cols(mine * HEADS + i)], qd.at[i, which, rows(h)], r_qd.at[i]).start()

    send_head(0)

    for copy in loads[2:]:
        copy.wait()
    lane = lax.broadcasted_iota(jnp.int32, (BLOCK, 2 * BLOCK), 1)

    def inner(j, total):
        part = jnp.sum(dov[:, cols(j)].astype(F32) * atv[:, cols(j)].astype(F32), axis=1, keepdims=True)
        return jnp.where(lane == j, part, total)

    deltas = lax.fori_loop(0, HQ, inner, jnp.zeros((BLOCK, 2 * BLOCK), F32), unroll=8)
    stats = jnp.where(lane < BLOCK, deltas, jnp.concatenate([ln[...], ln[...]], axis=1) * LOG2E).T
    stats = jnp.concatenate([stats[:HQ], stats[HQ:]], axis=1)
    for d in range(N):
        st_s[d] = stats[d * HEADS : (d + 1) * HEADS]

    @pl.loop(1, N)
    def _(s):
        d = lax.rem(h + s, N)
        remote(st_s.at[lax.rem(d + shift, N)], st_r.at[h], s_st, r_st, head=d).start()

    pltpu.make_async_copy(st_s.at[mine], st_r.at[h], r_st).start()

    wait(own.at[0], r_kv)
    forward = remote(own.at[m], own.at[m], s_fw, r_fw, head=mate)
    forward.start()
    onward = remote(own.at[m], prev.at[m], s_ctx, r_ctx, head=h_after, ctx=after)
    onward.start()

    @pl.loop(1, HEADS)
    def _(i):
        send_head(i)

    forward.wait_recv()
    own_t[...] = transposed(own[0])

    wait(st_r, r_st)
    for pair in range(N // 2):
        a, b = st_r[2 * pair], st_r[2 * pair + 1]
        at_pair = slice(pair * 2 * BLOCK, (pair + 1) * 2 * BLOCK)
        srow[:HEADS, at_pair] = jnp.concatenate([a[:, BLOCK:], b[:, BLOCK:]], axis=1)
        srow[HEADS:, at_pair] = jnp.concatenate([a[:, :BLOCK], b[:, :BLOCK]], axis=1)

    acc_own[...] = jnp.zeros_like(acc_own)
    acc_prev[...] = jnp.zeros_like(acc_prev)
    acc_sel[...] = jnp.zeros_like(acc_sel)
    dq_t[...] = jnp.zeros_like(dq_t)
    early = bp[c] > bp[before]

    def take_prev():
        onward.wait_recv()
        copy = remote(prev.at[m], prev.at[m], s_fwp, r_fwp, head=mate)
        copy.start()
        copy.wait_recv()
        for which in range(2):
            sel[which] = jnp.where(early, prev[which, :HALF], prev[which, HALF:])
        prev_t[...] = transposed(prev[0, :HALF])
        sel_t[...] = transposed(sel[0])

    def add(ref, lo, size, dk, dv):
        ref[0, lo : lo + size] += dk
        ref[1, lo : lo + size] += dv

    def pieces(x):
        return x.reshape(-1, PIECES, BLOCK, HEAD_SIZE)

    def row(i, lo, size):
        return srow[pl.ds(i, 1), lo : lo + size], srow[pl.ds(HEADS + i, 1), lo : lo + size]

    def combined(which):
        chosen = acc_sel[which]
        zero = jnp.zeros_like(chosen)
        low = acc_prev[which] + jnp.where(early, chosen, zero)
        return low, jnp.where(early, zero, chosen)

    def other_group(i):
        n0, d0 = row(i, 0, HALF)
        n1, d1 = row(i, HALF, HALF)
        q_sel = jnp.where(early, qd[i, 0, :HALF], qd[i, 0, HALF:])
        do_sel = jnp.where(early, qd[i, 1, :HALF], qd[i, 1, HALF:])
        n_sel, d_sel = jnp.where(early, n0, n1), jnp.where(early, d0, d1)
        q1, do1 = qd[i, 0, HALF:], qd[i, 1, HALF:]

        def keep_sel(dq, dk, dv):
            add(acc_sel, 0, HALF, dk, dv)
            zero = jnp.zeros_like(dq)
            dq_t[i, :, :HALF] += jnp.where(early, dq, zero)
            dq_t[i, :, HALF:] += jnp.where(early, zero, dq)

        def keep_prev(dq, dk, dv):
            add(acc_prev, 0, HALF, dk, dv)
            dq_t[i, :, HALF:] += dq

        in_turn([
            ((sel[0], sel[1], q_sel, do_sel), (sel_t[...], q_sel, do_sel, n_sel, d_sel, False), keep_sel),
            ((prev[0, :HALF], prev[1, :HALF], q1, do1), (prev_t[...], q1, do1, n1, d1, False), keep_prev),
        ])

    def own_tile(i, k0, k1, q0, q1, diagonal):
        q, do = qd[i, 0, q0:q1], qd[i, 1, q0:q1]
        norm, delta = row(i, q0, q1 - q0)

        def keep(dq, dk, dv):
            add(acc_own, k0, k1 - k0, dk, dv)
            dq_t[i, :, q0:q1] += dq

        return (own[0, k0:k1], own[1, k0:k1], q, do), (own_t[:, k0:k1], q, do, norm, delta, diagonal), keep

    def own_group(i, between):
        in_turn([own_tile(i, 0, HALF, HALF, ROWS, False)])
        between()
        in_turn([
            own_tile(i, 0, QUARTER, 0, HALF, True),
            own_tile(i, QUARTER, HALF, QUARTER, HALF, True),
            own_tile(i, HALF, HALF + QUARTER, HALF, ROWS, True),
            own_tile(i, HALF + QUARTER, ROWS, HALF + QUARTER, ROWS, True),
        ])

    @pl.loop(0, 2 * HEADS)
    def _(t):
        i = jnp.where(t < 4, lax.rem(t, 2), lax.div(t, 2))
        first = (t < 2) | (t == 4) | (t == 6)
        is_own = (t < 2) | (t == 4) | (t == 7)

        @pl.when(first)
        def _():
            wait(qd.at[i], r_qd.at[i])

        @pl.when(t == 2)
        def _():
            take_prev()

        @pl.when(jnp.logical_not(is_own))
        def _():
            other_group(i)

        @pl.when(t == 6)
        def _():
            low, high = combined(1 - m)
            x_s[:HALF] = low.astype(BF16)
            x_s[HALF:] = high.astype(BF16)
            remote(x_s, x_r, s_x, r_x, head=mate).start()

        def send_back():
            @pl.when(t == 7)
            def _():
                wait(x_r, r_x)
                low, high = combined(m)
                scale = jnp.where(m == 0, FACTOR, 1.0)
                low = pieces(((low + x_r[:HALF].astype(F32)) * scale).astype(BF16))
                high = pieces(((high + x_r[HALF:].astype(F32)) * scale).astype(BF16))
                for e in range(PIECES):
                    ctx_s[: N // PIECES // 2, e] = low[:, e]
                    ctx_s[N // PIECES // 2 :, e] = high[:, e]
                    remote(
                        ctx_s.at[:, e], ctx_r.at[:, e], s_back.at[e], r_back.at[e], head=h_before, ctx=before
                    ).start()

        @pl.when(is_own)
        def _():
            own_group(i, send_back)

        @pl.when(jnp.logical_not(first))
        def _():
            dq_s[i] = (dq_t[i] * FACTOR).T.astype(BF16)

            @pl.loop(1, N)
            def _(s):
                d = lax.rem(h + s, N)
                remote(dq_s.at[i, rows(d)], qg.at[:, cols(mine * HEADS + i)], s_dq, r_dq, head=d).start()

            pltpu.make_async_copy(dq_s.at[i, rows(h)], qg.at[:, cols(mine * HEADS + i)], r_dq).start()

    y_s[...] = acc_own[1 - m].astype(BF16)
    remote(y_s, y_r, s_y, r_y, head=mate).start()
    scale = jnp.where(m == 0, FACTOR, 1.0)
    wait(y_r, r_y)
    total = pieces((acc_own[m] + y_r[...].astype(F32)) * scale)
    for e in range(PIECES):
        wait(ctx_r.at[:, e], r_back.at[e])
        fin[:, e] = (total[:, e] + ctx_r[:, e].astype(F32)).astype(BF16)

        @pl.loop(0, N // PIECES)
        def _(s):
            t = lax.rem(lax.div(h, PIECES) + s, N // PIECES)
            d = t * PIECES + e

            @pl.when(d != h)
            def _():
                remote(fin.at[t, e], kvg.at[m, :, cols(g)], s_fin, r_fin, head=d).start()

            @pl.when(d == h)
            def _():
                pltpu.make_async_copy(fin.at[t, e], kvg.at[m, :, cols(g)], r_fin).start()

    most = (N - 1) * BLOCK
    wait(own.at[0, :most], s_kv)
    forward.wait_send()
    onward.wait_send()
    wait(prev.at[0], s_fwp)
    wait(st_r.at[: N - 1], s_st)
    for i in range(HEADS):
        wait(qd.at[i, :, :most], s_qd.at[i])
    wait(x_s, s_x)
    for e in range(PIECES):
        wait(ctx_s.at[:, e], s_back.at[e])
    wait(y_s, s_y)
    wait(dq_s.at[:, :most], s_dq)
    wait(own.at[0, :most], s_fin)
    wait(qg, r_dq)
    wait(kvg, r_fin)


def flush(qg, kvg, query_grad, key_gradient, value_gradient, sem):
    copies = [
        pltpu.make_async_copy(qg, query_grad, sem.at[0]),
        pltpu.make_async_copy(kvg.at[0], key_gradient, sem.at[1]),
        pltpu.make_async_copy(kvg.at[1], value_gradient, sem.at[2]),
    ]
    for copy in copies:
        copy.start()
    for copy in copies:
        copy.wait()


def shards(query_states, saved_key_rows, saved_value_rows, attn_output, out_grad, log_norm, block_pos):
    hbm = pl.BlockSpec(memory_space=pltpu.HBM)
    vmem = pl.BlockSpec(memory_space=pltpu.VMEM)
    inputs = (query_states, out_grad, attn_output, saved_key_rows, saved_value_rows, log_norm, block_pos)
    inputs = tuple(pltpu.with_memory_space_constraint(x, pltpu.HBM) for x in inputs)
    dma = pltpu.SemaphoreType.DMA
    half = lambda *lead: pltpu.VMEM((*lead, HALF, HEAD_SIZE), BF16)
    parts = pltpu.VMEM((N // PIECES, PIECES, BLOCK, HEAD_SIZE), BF16)
    full = lambda *lead: pltpu.VMEM((*lead, ROWS, HEAD_SIZE), BF16)
    qg, kvg = pl.pallas_call(
        kernel,
        out_shape=(
            pltpu.VMEM((BLOCK, HQ * HEAD_SIZE), BF16),
            pltpu.VMEM((2, BLOCK, KEY_VALUE_HEADS * HEAD_SIZE), BF16),
        ),
        in_specs=[hbm] * 7,
        out_specs=(vmem, vmem),
        scratch_shapes=[
            pltpu.VMEM((BLOCK, HQ), F32),
            pltpu.SMEM((N * N,), jnp.int32),
            pltpu.VMEM((BLOCK, HQ * HEAD_SIZE), BF16),
            pltpu.VMEM((BLOCK, HQ * HEAD_SIZE), BF16),
            pltpu.VMEM((2, BLOCK, KEY_VALUE_HEADS * HEAD_SIZE), BF16),
            pltpu.VMEM((N, HEADS, 2 * BLOCK), F32),
            pltpu.VMEM((N, HEADS, 2 * BLOCK), F32),
            pltpu.VMEM((2 * HEADS, ROWS), F32),
            full(HEADS, 2),
            full(2),
            full(2),
            pltpu.VMEM((HEAD_SIZE, ROWS), BF16),
            pltpu.VMEM((HEAD_SIZE, HALF), BF16),
            half(2),
            pltpu.VMEM((HEAD_SIZE, HALF), BF16),
            pltpu.VMEM((2, ROWS, HEAD_SIZE), F32),
            pltpu.VMEM((2, HALF, HEAD_SIZE), F32),
            pltpu.VMEM((2, HALF, HEAD_SIZE), F32),
            pltpu.VMEM((HEADS, HEAD_SIZE, ROWS), F32),
            full(HEADS),
            full(),
            full(),
            parts,
            parts,
            full(),
            full(),
            parts,
            dma((6,)),
            dma, dma, dma, dma, dma, dma, dma, dma, dma, dma,
            dma((HEADS,)), dma((HEADS,)),
            dma, dma, dma((PIECES,)), dma((PIECES,)), dma, dma, dma, dma, dma, dma,
        ],
        compiler_params=pltpu.CompilerParams(
            collective_id=1, has_side_effects=True, vmem_limit_bytes=48 << 20
        ),
        name="attention_backward",
    )(*inputs)
    return pl.pallas_call(
        flush,
        out_shape=(
            pltpu.HBM((BLOCK, HQ * HEAD_SIZE), BF16),
            pltpu.HBM((BLOCK, KEY_VALUE_HEADS * HEAD_SIZE), BF16),
            pltpu.HBM((BLOCK, KEY_VALUE_HEADS * HEAD_SIZE), BF16),
        ),
        in_specs=[vmem] * 2,
        out_specs=(hbm,) * 3,
        scratch_shapes=[dma((3,))],
        name="store_results",
    )(*(pltpu.with_memory_space_constraint(x, pltpu.VMEM) for x in (qg, kvg)))


def solution(mesh):
    tokens = P(("head", "ctx"), None)
    return jax.shard_map(
        shards,
        mesh=mesh,
        in_specs=(tokens,) * 6 + (P(),),
        out_specs=(tokens,) * 3,
        check_vma=False,
    )
```

time: 57.4 us -> 52.9 us (0.922)
  the two profiles are of different devices: /device:TPU:1 before, /device:TPU:109 now
where the time goes in v2:
time: 52.9 us; the launch traced here: 52.8 us
  Pallas kernels  52.1 us (98%)
  between operations  0.64 us (1%)
    pallas_call x1, Pallas kernels, shards(): pl.pallas_call(kernel, out_shape=(pltpu.VMEM((BLOCK, HQ * HEAD_SIZE), BF1...  51.1 us
    pallas_call x1, Pallas kernels, shards(): pl.pallas_call(flush, out_shape=(pltpu.HBM((BLOCK, HQ * HEAD_SIZE), BF16)...  1.07 us

profile of v2, /device:TPU:109, one launch (start us, length us, event | category | flops | bytes accessed | tf_op | source)
XLA Modules:
  0.0 52.8 jit_solution(11598124867427877249)
XLA Ops:
  0.6 51.1 %attention_backward.1 = (bf16[64,8192]{1,0:T(8,128)(2,1)S(1)}, bf16[2,64,1024]{2,1,0:T(8,128)(2,1)S(1)}) custom-call(bf16[64,8192]{1,0:T(8,128)(2,1)} %q.1, bf16[64,8192]{1,0:T(8,128)(2,1)} %do.1, bf16[64,8192]{1,0:T(8,128)(2,1)} %at.1, bf16[64,1024]{1,0:T(8,128)(2,1)} %k.1, bf16[64,1024]{1,0:T(8,128)(2,1)} %v.1, f32[64,64]{1,0:T(8,128)} %log_norm.1, ...), custom_call_target="tpu_custom_call" | custom-call | tf_op jit(solution)/shard_map/attention_backward/pallas_call | solution.py:374
  51.7 1.1 %store_results.1 = (bf16[64,8192]{1,0:T(8,128)(2,1)}, bf16[64,1024]{1,0:T(8,128)(2,1)}, bf16[64,1024]{1,0:T(8,128)(2,1)}) custom-call(bf16[64,8192]{1,0:T(8,128)(2,1)S(1)} %get-tuple-element.5.qg, bf16[2,64,1024]{2,1,0:T(8,128)(2,1)S(1)} %get-tuple-element.6.kvg), custom_call_target="tpu_custom_call" | custom-call | tf_op jit(solution)/shard_map/store_results/pallas_call | solution.py:420

commit v3 on v2

--- a/solution.py
+++ b/solution.py
@@ -31,7 +31,7 @@
 
 
 def transposed(x):
-    return x.astype(F32).T.astype(BF16)
+    return x.T
 
 
 def scores(k, v, q, do):
@@ -65,7 +65,7 @@
     q, do, at, k, v, log_norm, block_pos,
     qg, kvg,
     ln, bp, dov, atv, kvs, st_s, st_r, srow, qd, own, prev, own_t, prev_t, sel, sel_t,
-    acc_own, acc_prev, acc_sel, dq_t, dq_s, x_s, x_r, ctx_s, ctx_r, y_s, y_r, fin,
+    acc_own, acc_prev, acc_sel, dq_t, dq_s, x_s, x_r, back_s, back_r, ctx_s, ctx_r, y_s, y_r, fin,
     s_load, s_kv, r_kv, s_fw, r_fw, s_ctx, r_ctx, s_fwp, r_fwp, s_st, r_st, s_qd, r_qd,
     s_x, r_x, s_back, r_back, s_y, r_y, s_dq, r_dq, s_fin, r_fin,
 ):
@@ -186,11 +186,11 @@
     dq_t[...] = jnp.zeros_like(dq_t)
     early = bp[c] > bp[before]
 
+    def share_prev():
+        return remote(prev.at[m], prev.at[m], s_fwp, r_fwp, head=mate)
+
     def take_prev():
-        onward.wait_recv()
-        copy = remote(prev.at[m], prev.at[m], s_fwp, r_fwp, head=mate)
-        copy.start()
-        copy.wait_recv()
+        share_prev().wait_recv()
         for which in range(2):
             sel[which] = jnp.where(early, prev[which, :HALF], prev[which, HALF:])
         prev_t[...] = transposed(prev[0, :HALF])
@@ -206,13 +206,15 @@
     def row(i, lo, size):
         return srow[pl.ds(i, 1), lo : lo + size], srow[pl.ds(HEADS + i, 1), lo : lo + size]
 
-    def combined(which):
-        chosen = acc_sel[which]
-        zero = jnp.zeros_like(chosen)
-        low = acc_prev[which] + jnp.where(early, chosen, zero)
-        return low, jnp.where(early, zero, chosen)
-
-    def other_group(i):
+    def swap(n):
+        return remote(x_s.at[n], x_r.at[n], s_x.at[n], r_x.at[n], head=mate)
+
+    def both_cores(ref, n):
+        wait(x_r.at[n], r_x.at[n])
+        scale = jnp.where(m == 0, FACTOR, 1.0)
+        return ((ref[m] + x_r[n].astype(F32)) * scale).astype(BF16)
+
+    def other_tiles(i):
         n0, d0 = row(i, 0, HALF)
         n1, d1 = row(i, HALF, HALF)
         q_sel = jnp.where(early, qd[i, 0, :HALF], qd[i, 0, HALF:])
@@ -230,10 +232,10 @@
             add(acc_prev, 0, HALF, dk, dv)
             dq_t[i, :, HALF:] += dq
 
-        in_turn([
+        return (
+            ((prev[0, :HALF], prev[1, :HALF], q1, do1), (prev_t[...], q1, do1, n1, d1, False), keep_prev),
             ((sel[0], sel[1], q_sel, do_sel), (sel_t[...], q_sel, do_sel, n_sel, d_sel, False), keep_sel),
-            ((prev[0, :HALF], prev[1, :HALF], q1, do1), (prev_t[...], q1, do1, n1, d1, False), keep_prev),
-        ])
+        )
 
     def own_tile(i, k0, k1, q0, q1, diagonal):
         q, do = qd[i, 0, q0:q1], qd[i, 1, q0:q1]
@@ -245,16 +247,26 @@
 
         return (own[0, k0:k1], own[1, k0:k1], q, do), (own_t[:, k0:k1], q, do, norm, delta, diagonal), keep
 
-    def own_group(i, between):
-        in_turn([own_tile(i, 0, HALF, HALF, ROWS, False)])
-        between()
+    def own_group(i):
         in_turn([
+            own_tile(i, 0, HALF, HALF, ROWS, False),
             own_tile(i, 0, QUARTER, 0, HALF, True),
             own_tile(i, QUARTER, HALF, QUARTER, HALF, True),
             own_tile(i, HALF, HALF + QUARTER, HALF, ROWS, True),
             own_tile(i, HALF + QUARTER, ROWS, HALF + QUARTER, ROWS, True),
         ])
 
+    def round_dq(i):
+        dq_s[i] = (dq_t[i] * FACTOR).astype(BF16).T
+
+    def send_dq(i):
+        @pl.loop(1, N)
+        def _(s):
+            d = lax.rem(h + s, N)
+            remote(dq_s.at[i, rows(d)], qg.at[:, cols(mine * HEADS + i)], s_dq, r_dq, head=d).start()
+
+        pltpu.make_async_copy(dq_s.at[i, rows(h)], qg.at[:, cols(mine * HEADS + i)], r_dq).start()
+
     @pl.loop(0, 2 * HEADS)
     def _(t):
         i = jnp.where(t < 4, lax.rem(t, 2), lax.div(t, 2))
@@ -265,59 +277,60 @@
         def _():
             wait(qd.at[i], r_qd.at[i])
 
+        @pl.when(t == 1)
+        def _():
+            onward.wait_recv()
+            share_prev().start()
+
         @pl.when(t == 2)
         def _():
             take_prev()
 
-        @pl.when(jnp.logical_not(is_own))
-        def _():
-            other_group(i)
+        @pl.when(jnp.logical_not(is_own | (t == 6)))
+        def _():
+            in_turn(other_tiles(i))
 
         @pl.when(t == 6)
         def _():
-            low, high = combined(1 - m)
-            x_s[:HALF] = low.astype(BF16)
-            x_s[HALF:] = high.astype(BF16)
-            remote(x_s, x_r, s_x, r_x, head=mate).start()
-
-        def send_back():
-            @pl.when(t == 7)
-            def _():
-                wait(x_r, r_x)
-                low, high = combined(m)
-                scale = jnp.where(m == 0, FACTOR, 1.0)
-                low = pieces(((low + x_r[:HALF].astype(F32)) * scale).astype(BF16))
-                high = pieces(((high + x_r[HALF:].astype(F32)) * scale).astype(BF16))
-                for e in range(PIECES):
-                    ctx_s[: N // PIECES // 2, e] = low[:, e]
-                    ctx_s[N // PIECES // 2 :, e] = high[:, e]
-                    remote(
-                        ctx_s.at[:, e], ctx_r.at[:, e], s_back.at[e], r_back.at[e], head=h_before, ctx=before
-                    ).start()
+            for n, (spec, ref) in enumerate(zip(other_tiles(i), (acc_prev, acc_sel))):
+                in_turn([spec])
+                x_s[n] = ref[1 - m].astype(BF16)
+                swap(n).start()
+            back_s[...] = both_cores(acc_prev, 0)
+            remote(back_s, back_r, s_back.at[PIECES], r_back.at[PIECES], head=h_before, ctx=before).start()
+            round_dq(i - 1)
+            chosen = pieces(both_cores(acc_sel, 1))
+            for e in range(PIECES):
+                ctx_s[:, e] = chosen[:, e]
+                remote(
+                    ctx_s.at[:, e], ctx_r.at[:, e], s_back.at[e], r_back.at[e], head=h_before, ctx=before
+                ).start()
+            send_dq(i - 1)
 
         @pl.when(is_own)
         def _():
-            own_group(i, send_back)
-
-        @pl.when(jnp.logical_not(first))
-        def _():
-            dq_s[i] = (dq_t[i] * FACTOR).T.astype(BF16)
-
-            @pl.loop(1, N)
-            def _(s):
-                d = lax.rem(h + s, N)
-                remote(dq_s.at[i, rows(d)], qg.at[:, cols(mine * HEADS + i)], s_dq, r_dq, head=d).start()
-
-            pltpu.make_async_copy(dq_s.at[i, rows(h)], qg.at[:, cols(mine * HEADS + i)], r_dq).start()
+            own_group(i)
+
+        @pl.when(jnp.logical_not(first | (t == 5)))
+        def _():
+            round_dq(i)
+            send_dq(i)
 
     y_s[...] = acc_own[1 - m].astype(BF16)
     remote(y_s, y_r, s_y, r_y, head=mate).start()
     scale = jnp.where(m == 0, FACTOR, 1.0)
     wait(y_r, r_y)
     total = pieces((acc_own[m] + y_r[...].astype(F32)) * scale)
+    next_early = bp[after] > bp[c]
+    wait(back_r, r_back.at[PIECES])
+    low = total[: N // PIECES // 2] + pieces(back_r[...]).astype(F32)
+    high = total[N // PIECES // 2 :]
     for e in range(PIECES):
         wait(ctx_r.at[:, e], r_back.at[e])
-        fin[:, e] = (total[:, e] + ctx_r[:, e].astype(F32)).astype(BF16)
+        chosen = ctx_r[:, e].astype(F32)
+        zero = jnp.zeros_like(chosen)
+        fin[: N // PIECES // 2, e] = (low[:, e] + jnp.where(next_early, chosen, zero)).astype(BF16)
+        fin[N // PIECES // 2 :, e] = (high[:, e] + jnp.where(next_early, zero, chosen)).astype(BF16)
 
         @pl.loop(0, N // PIECES)
         def _(s):
@@ -340,7 +353,9 @@
     wait(st_r.at[: N - 1], s_st)
     for i in range(HEADS):
         wait(qd.at[i, :, :most], s_qd.at[i])
-    wait(x_s, s_x)
+    for n in range(2):
+        wait(x_s.at[n], s_x.at[n])
+    wait(back_s, s_back.at[PIECES])
     for e in range(PIECES):
         wait(ctx_s.at[:, e], s_back.at[e])
     wait(y_s, s_y)
@@ -400,17 +415,19 @@
             pltpu.VMEM((2, HALF, HEAD_SIZE), F32),
             pltpu.VMEM((HEADS, HEAD_SIZE, ROWS), F32),
             full(HEADS),
-            full(),
-            full(),
-            parts,
-            parts,
+            half(2),
+            half(2),
+            half(),
+            half(),
+            pltpu.VMEM((N // PIECES // 2, PIECES, BLOCK, HEAD_SIZE), BF16),
+            pltpu.VMEM((N // PIECES // 2, PIECES, BLOCK, HEAD_SIZE), BF16),
             full(),
             full(),
             parts,
             dma((6,)),
             dma, dma, dma, dma, dma, dma, dma, dma, dma, dma,
             dma((HEADS,)), dma((HEADS,)),
-            dma, dma, dma((PIECES,)), dma((PIECES,)), dma, dma, dma, dma, dma, dma,
+            dma((2,)), dma((2,)), dma((PIECES + 1,)), dma((PIECES + 1,)), dma, dma, dma, dma, dma, dma,
         ],
         compiler_params=pltpu.CompilerParams(
             collective_id=1, has_side_effects=True, vmem_limit_bytes=48 << 20

time: 52.9 us -> 51.7 us (0.977)
  the two profiles are of different devices: /device:TPU:109 before, /device:TPU:1 now
where the time goes in v3:
time: 51.7 us; the launch traced here: 51.6 us
  Pallas kernels  50.9 us (98%)
  between operations  0.64 us (1%)
    pallas_call x1, Pallas kernels, shards(): pl.pallas_call(kernel, out_shape=(pltpu.VMEM((BLOCK, HQ * HEAD_SIZE), BF1...  49.8 us
    pallas_call x1, Pallas kernels, shards(): pl.pallas_call(flush, out_shape=(pltpu.HBM((BLOCK, HQ * HEAD_SIZE), BF16)...  1.07 us

profile of v3, /device:TPU:1, one launch (start us, length us, event | category | flops | bytes accessed | tf_op | source)
XLA Modules:
  0.0 51.6 jit_solution(510839571520872980)
XLA Ops:
  0.6 49.8 %attention_backward.1 = (bf16[64,8192]{1,0:T(8,128)(2,1)S(1)}, bf16[2,64,1024]{2,1,0:T(8,128)(2,1)S(1)}) custom-call(bf16[64,8192]{1,0:T(8,128)(2,1)} %q.1, bf16[64,8192]{1,0:T(8,128)(2,1)} %do.1, bf16[64,8192]{1,0:T(8,128)(2,1)} %at.1, bf16[64,1024]{1,0:T(8,128)(2,1)} %k.1, bf16[64,1024]{1,0:T(8,128)(2,1)} %v.1, f32[64,64]{1,0:T(8,128)} %log_norm.1, ...), custom_call_target="tpu_custom_call" | custom-call | tf_op jit(solution)/shard_map/attention_backward/pallas_call | solution.py:389
  50.5 1.1 %store_results.1 = (bf16[64,8192]{1,0:T(8,128)(2,1)}, bf16[64,1024]{1,0:T(8,128)(2,1)}, bf16[64,1024]{1,0:T(8,128)(2,1)}) custom-call(bf16[64,8192]{1,0:T(8,128)(2,1)S(1)} %get-tuple-element.5.qg, bf16[2,64,1024]{2,1,0:T(8,128)(2,1)S(1)} %get-tuple-element.6.kvg), custom_call_target="tpu_custom_call" | custom-call | tf_op jit(solution)/shard_map/store_results/pallas_call | solution.py:437

commit v4 on v3

--- a/solution.py
+++ b/solution.py
@@ -15,11 +15,17 @@
 HALF = ROWS // 2
 QUARTER = ROWS // 4
 PIECES = 4
+ORDER = [(x, y, c) for x, y in ((1, 2), (0, 2), (1, 1), (1, 3), (0, 1), (0, 3), (1, 0)) for c in (0, 1)] + [(0, 0, 1)]
 FACTOR = HEAD_SIZE**-0.5
 LOG2E = 1.4426950408889634
 MESH = pl.DeviceIdType.MESH
 F32 = jnp.float32
 BF16 = jnp.bfloat16
+
+
+def every(f):
+    for s in range(1, N):
+        f(s)
 
 
 def dot(a, b):
@@ -89,6 +95,12 @@
     def wait(ref, sem):
         pltpu.make_async_copy(ref, ref, sem).wait()
 
+    def partner(s):
+        x, y, core = ORDER[s - 1]
+        chip_y = lax.rem(lax.rem(lax.div(h, 2), 4) + y, 4)
+        chip_x = lax.rem(lax.div(h, 8) + x, 2)
+        return chip_x * 8 + chip_y * 2 + lax.rem(h + core, 2)
+
     def cols(j):
         return pl.ds(pl.multiple_of(j * HEAD_SIZE, HEAD_SIZE), HEAD_SIZE)
 
@@ -117,18 +129,18 @@
     loads[1].wait()
     pl.semaphore_wait(barrier, N)
 
-    @pl.loop(1, N)
+    @every
     def _(s):
-        d = lax.rem(h + s, N)
+        d = partner(s)
         e = lax.rem(d, 2)
         remote(kvs.at[e, :, cols(lax.div(lax.rem(d + shift, N), 2))], own.at[e, rows(h)], s_kv, r_kv, head=d).start()
 
     pltpu.make_async_copy(kvs.at[m, :, cols(g)], own.at[m, rows(h)], r_kv).start()
 
     def send_head(i):
-        @pl.loop(1, N)
+        @every
         def _(s):
-            d = lax.rem(h + s, N)
+            d = partner(s)
             for which, ref in ((0, q), (1, do)):
                 remote(
                     ref.at[:, cols(lax.rem(d + shift, N) * HEADS + i)], qd.at[i, which, rows(h)], s_qd.at[i], r_qd.at[i], head=d
@@ -153,9 +165,9 @@
     for d in range(N):
         st_s[d] = stats[d * HEADS : (d + 1) * HEADS]
 
-    @pl.loop(1, N)
+    @every
     def _(s):
-        d = lax.rem(h + s, N)
+        d = partner(s)
         remote(st_s.at[lax.rem(d + shift, N)], st_r.at[h], s_st, r_st, head=d).start()
 
     pltpu.make_async_copy(st_s.at[mine], st_r.at[h], r_st).start()
@@ -260,9 +272,9 @@
         dq_s[i] = (dq_t[i] * FACTOR).astype(BF16).T
 
     def send_dq(i):
-        @pl.loop(1, N)
+        @every
         def _(s):
-            d = lax.rem(h + s, N)
+            d = partner(s)
             remote(dq_s.at[i, rows(d)], qg.at[:, cols(mine * HEADS + i)], s_dq, r_dq, head=d).start()
 
         pltpu.make_async_copy(dq_s.at[i, rows(h)], qg.at[:, cols(mine * HEADS + i)], r_dq).start()
@@ -334,7 +346,7 @@
 
         @pl.loop(0, N // PIECES)
         def _(s):
-            t = lax.rem(lax.div(h, PIECES) + s, N // PIECES)
+            t = lax.rem(lax.div(h, PIECES) + (N // PIECES - 1) - s, N // PIECES)
             d = t * PIECES + e
 
             @pl.when(d != h)

time: 51.7 us -> 50.6 us (0.979)
  Pallas kernels: 50.9 us -> 49.4 us
    pallas_call x1, Pallas kernels: 49.8 us -> 48.4 us  [shards(): pl.pallas_call(kernel, out_shape=(pltpu.VMEM((BLOCK, HQ * HEAD_SIZE), BF1...]
where the time goes in v4:
time: 50.6 us; the launch traced here: 50.1 us
  Pallas kernels  49.4 us (98%)
  between operations  0.64 us (1%)
    pallas_call x1, Pallas kernels, shards(): pl.pallas_call(kernel, out_shape=(pltpu.VMEM((BLOCK, HQ * HEAD_SIZE), BF1...  48.4 us
    pallas_call x1, Pallas kernels, shards(): pl.pallas_call(flush, out_shape=(pltpu.HBM((BLOCK, HQ * HEAD_SIZE), BF16)...  1.07 us

profile of v4, /device:TPU:1, one launch (start us, length us, event | category | flops | bytes accessed | tf_op | source)
XLA Modules:
  0.0 50.1 jit_solution(16215816323154069421)
XLA Ops:
  0.6 48.4 %attention_backward.1 = (bf16[64,8192]{1,0:T(8,128)(2,1)S(1)}, bf16[2,64,1024]{2,1,0:T(8,128)(2,1)S(1)}) custom-call(bf16[64,8192]{1,0:T(8,128)(2,1)} %q.1, bf16[64,8192]{1,0:T(8,128)(2,1)} %do.1, bf16[64,8192]{1,0:T(8,128)(2,1)} %at.1, bf16[64,1024]{1,0:T(8,128)(2,1)} %k.1, bf16[64,1024]{1,0:T(8,128)(2,1)} %v.1, f32[64,64]{1,0:T(8,128)} %log_norm.1, ...), custom_call_target="tpu_custom_call" | custom-call | tf_op jit(solution)/shard_map/attention_backward/pallas_call | solution.py:401
  49.0 1.1 %store_results.1 = (bf16[64,8192]{1,0:T(8,128)(2,1)}, bf16[64,1024]{1,0:T(8,128)(2,1)}, bf16[64,1024]{1,0:T(8,128)(2,1)}) custom-call(bf16[64,8192]{1,0:T(8,128)(2,1)S(1)} %get-tuple-element.5.qg, bf16[2,64,1024]{2,1,0:T(8,128)(2,1)S(1)} %get-tuple-element.6.kvg), custom_call_target="tpu_custom_call" | custom-call | tf_op jit(solution)/shard_map/store_results/pallas_call | solution.py:449

commit v5 on v4

--- a/solution.py
+++ b/solution.py
@@ -14,7 +14,7 @@
 ROWS = N * BLOCK
 HALF = ROWS // 2
 QUARTER = ROWS // 4
-PIECES = 4
+PIECES = 8
 ORDER = [(x, y, c) for x, y in ((1, 2), (0, 2), (1, 1), (1, 3), (0, 1), (0, 3), (1, 0)) for c in (0, 1)] + [(0, 0, 1)]
 FACTOR = HEAD_SIZE**-0.5
 LOG2E = 1.4426950408889634

time: 50.6 us -> 50.5 us (level)
  no operation moved by 1% of the time
where the time goes in v5:
time: 50.5 us; the launch traced here: 49.7 us
  Pallas kernels  49 us (97%)
  between operations  0.64 us (1%)
    pallas_call x1, Pallas kernels, shards(): pl.pallas_call(kernel, out_shape=(pltpu.VMEM((BLOCK, HQ * HEAD_SIZE), BF1...  47.9 us
    pallas_call x1, Pallas kernels, shards(): pl.pallas_call(flush, out_shape=(pltpu.HBM((BLOCK, HQ * HEAD_SIZE), BF16)...  1.07 us

profile of v5, /device:TPU:1, one launch (start us, length us, event | category | flops | bytes accessed | tf_op | source)
XLA Modules:
  0.0 49.7 jit_solution(9297988168359314973)
XLA Ops:
  0.6 47.9 %attention_backward.1 = (bf16[64,8192]{1,0:T(8,128)(2,1)S(1)}, bf16[2,64,1024]{2,1,0:T(8,128)(2,1)S(1)}) custom-call(bf16[64,8192]{1,0:T(8,128)(2,1)} %q.1, bf16[64,8192]{1,0:T(8,128)(2,1)} %do.1, bf16[64,8192]{1,0:T(8,128)(2,1)} %at.1, bf16[64,1024]{1,0:T(8,128)(2,1)} %k.1, bf16[64,1024]{1,0:T(8,128)(2,1)} %v.1, f32[64,64]{1,0:T(8,128)} %log_norm.1, ...), custom_call_target="tpu_custom_call" | custom-call | tf_op jit(solution)/shard_map/attention_backward/pallas_call | solution.py:401
  48.6 1.1 %store_results.1 = (bf16[64,8192]{1,0:T(8,128)(2,1)}, bf16[64,1024]{1,0:T(8,128)(2,1)}, bf16[64,1024]{1,0:T(8,128)(2,1)}) custom-call(bf16[64,8192]{1,0:T(8,128)(2,1)S(1)} %get-tuple-element.5.qg, bf16[2,64,1024]{2,1,0:T(8,128)(2,1)S(1)} %get-tuple-element.6.kvg), custom_call_target="tpu_custom_call" | custom-call | tf_op jit(solution)/shard_map/store_results/pallas_call | solution.py:449
